TPU v7x, 256 devices: a whole 4x4x8 slice. The times are simulated.
256 devices in a mesh: space: 16 (over z, core), basis: 16 (over y, x).
Axes of the slice: x: 4, y: 4, z: 8, core: 2. Of those that a mesh axis runs over, the one named last changes fastest.
Arguments:
- basis_block: float32 [512, 196608], P('basis', 'space'), may hold values from -6 to 6
- schur: float32 [512, 512], P(('space', 'basis')), may hold values from -0.25 to 0.25
- kept: int32 [256], replicated, may hold values from 0 to 511, as said below
Outputs:
- rotated: float32 [256, 196608], P('basis', 'space')
Inputs may be any that keep to these rules, and one draw needn't show every extreme that they name: `kept`: 256 different column indices; 0 and 511 are always among them.
All inputs are finite; a program needn't handle non-finite values.
Results may differ from a plain program's by a relative error of at most 0.00007.
Values sent between devices are 32-bit elements; how exact they have to be, the bound alone decides.
A program may use at most 128 MiB of HBM per device.

v0:
```python
import jax
import jax.numpy as jnp
from jax import lax
from jax.sharding import PartitionSpec as P


def body(basis_block, schur, kept):
    groups = lax.axis_size("basis")
    selected = jnp.take(schur, kept, axis=1)
    kept_full = lax.all_gather(selected, ("space", "basis"), axis=0, tiled=True)
    kept_cols = kept_full.shape[1]
    own_cols = kept_cols // groups
    mine = lax.dynamic_slice_in_dim(kept_full, lax.axis_index("basis") * own_cols, own_cols, 1).T
    return jnp.dot(
        mine,
        lax.all_gather(basis_block, "basis", axis=0, tiled=True),
        precision=lax.Precision.HIGHEST,
        preferred_element_type=jnp.float32,
    )


def solution(mesh):
    in_specs = (P("basis", "space"), P(("space", "basis"), None), P())
    out_specs = P("basis", "space")
    return jax.shard_map(body, mesh=mesh, in_specs=in_specs, out_specs=out_specs, check_vma=False)
```

profile of v0, /device:TPU:1, one launch (start us, length us, event | category | flops | bytes accessed | tf_op | source)
XLA Modules:
  0.0 199.3 jit_solution(13863430865283513537)
XLA Ops:
  6.5 0.0 all-gather.3.cloned.1.call-start
  6.5 0.7 all-gather.3.cloned.1.call-update
  7.3 0.8 copy.7
  8.1 0.7 compare_select_fusion
  8.8 0.7 gather_fusion
  9.5 0.7 compare_and_fusion
  10.2 0.1 select_bitcast_fusion
  10.3 0.1 copy.8
  10.4 128.2 %all-gather = f32[256,2,256]{2,1,0:T(2,128)S(1)} all-gather(f32[1,2,256]{2,1,0:T(2,128)S(1)} %copy.8), channel_id=1, replica_groups=mesh['space'=16,'basis'=16] {'space','basis'}, dimensions={0}, use_global_device_ids=true | all-gather | bytes 526336 | tf_op jit(solution)/shard_map/all_gather | solution.py:10
  138.6 0.4 reshape.15
  139.0 36.0 %all-gather.3.cloned.1.call-done = f32[512,12288]{1,0:T(8,128)} async-done(((f32[32,12288]{1,0:T(8,128)}), f32[512,12288]{1,0:T(8,128)}) %all-gather.3.cloned.1.call-update) | async-done | bytes 25165840 | tf_op jit(solution)/shard_map/all_gather | solution.py:16
  174.9 17.5 %fusion = f32[16,12288]{1,0:T(8,128)} fusion(f32[512,12288]{1,0:T(8,128)} %all-gather.3.cloned.1.call-done, f32[512,256]{1,0:T(8,128)S(1)} %reshape.15, s32[]{:T(128)S(6)} %select_n.14), kind=kOutput, calls=%fused_computation.1 | convolution fusion | flops 1207959552 | bytes 26214404 | tf_op jit(solution)/shard_map/dot_general | solution.py:14
  (1 shorter events, 0.0 us)
Async XLA Ops:
  6.5 168.4 %all-gather.3.cloned.1.call-start = ((), (), s32[]{:S(2)}) async-start(), calls=%async_computation | async-start | bytes 26738688 | tf_op jit(solution)/shard_map/all_gather | solution.py:16
Sparse Core Ops, SparseCore 0:
  9.8 165.0 all-gather.2
where the time goes:
time: 199 us
  blocking collectives  128 us (64%)
  waiting for transfers between devices  36.7 us (18%)
  matrix products  17.5 us (9%)
  between operations  13.4 us (7%)
  local copies, waits for them, and re-layouts  1.99 us (1%)
    all_gather x1, blocking collectives, body(): kept_full = lax.all_gather(selected, ('space', 'basis'), axis=0, tiled=True)  128 us
    all_gather x1, waiting for transfers between devices, body(): lax.all_gather(basis_block, 'basis', axis=0, tiled=True)  36 us
    dot_general x1, matrix products, body(): jnp.dot(mine, lax.all_gather(basis_block, 'basis', axis=0, tiled=True), p...  17.5 us
  transfers between devices with their start and end apart: 1, of which 1 were waited for; matrix products, arithmetic and copies ran while one was open for 2% of the time, Pallas kernels for 0%

commit v1 on v0

v1 whole, which is shorter than its diff:
```python
import jax
import jax.numpy as jnp
from jax import lax
from jax.sharding import PartitionSpec as P


def body(basis_block, schur, kept):
    selected = jnp.take(schur, kept, axis=1)
    kept_full = lax.all_gather(selected, ("space", "basis"), axis=0, tiled=True)
    columns = lax.all_to_all(basis_block, "basis", split_axis=1, concat_axis=0, tiled=True)
    product = jnp.dot(
        kept_full.T,
        columns,
        precision=lax.Precision.HIGHEST,
        preferred_element_type=jnp.float32,
    )
    return lax.all_to_all(product, "basis", split_axis=0, concat_axis=1, tiled=True)


def solution(mesh):
    in_specs = (P("basis", "space"), P(("space", "basis"), None), P())
    out_specs = P("basis", "space")
    return jax.shard_map(body, mesh=mesh, in_specs=in_specs, out_specs=out_specs, check_vma=False)
```

time: 199 us -> 164 us (0.82)
  waiting for transfers between devices: 36.7 us -> 0.01 us
  blocking collectives: 128 us -> 149 us
  matrix products: 17.5 us -> 1.48 us
  between operations: 13.4 us -> 0.09 us
  starting transfers between devices: 0.01 us -> 7.72 us
  local copies, waits for them, and re-layouts: 1.99 us -> 5.19 us
    all_gather x1 -> x0, waiting for transfers between devices: 36 us -> none  [body(): lax.all_gather(basis_block, 'basis', axis=0, tiled=True)]
    all_to_all x0 -> x1, blocking collectives: none -> 16.6 us  [body(): lax.all_to_all(product, 'basis', split_axis=0, concat_axis=1, tiled=True)]
    dot_general x1, matrix products: 17.5 us -> 1.48 us  [body(): jnp.dot(kept_full.T, columns, precision=lax.Precision.HIGHEST, preferred_...]
    all_to_all x0 -> x1, starting transfers between devices: none -> 7.72 us  [body(): lax.all_to_all(basis_block, 'basis', split_axis=1, concat_axis=0, tiled=T...]
    all_gather x1, blocking collectives: 128 us -> 132 us  [body(): kept_full = lax.all_gather(selected, ('space', 'basis'), axis=0, tiled=True)]
    all_to_all x0 -> x2, local copies, waits for them, and re-layouts: none -> 3.68 us  [the longest x1 2.74 us: body(): lax.all_to_all(basis_block, 'basis', split_axis=1, concat_axis=0, tiled=T...]
  transfers between devices with their start and end apart: 1 -> 1, of which waited for: 1 -> 0; matrix products, arithmetic and copies ran while one was open for 2% -> 1% of each run, Pallas kernels for 0% -> 0%
where the time goes in v1:
time: 164 us; the launch traced here: 163 us
  blocking collectives  149 us (91%)
  starting transfers between devices  7.72 us (5%)
  local copies, waits for them, and re-layouts  5.19 us (3%)
    all_gather x1, blocking collectives, body(): kept_full = lax.all_gather(selected, ('space', 'basis'), axis=0, tiled=True)  132 us
    all_to_all x1, blocking collectives, body(): lax.all_to_all(product, 'basis', split_axis=0, concat_axis=1, tiled=True)  16.6 us
    all_to_all x1, starting transfers between devices, body(): lax.all_to_all(basis_block, 'basis', split_axis=1, concat_axis=0, tiled=T...  7.72 us
  transfers between devices with their start and end apart: 1, of which 0 were waited for; matrix products, arithmetic and copies ran while one was open for 1% of the time, Pallas kernels for 0%

profile of v1, /device:TPU:1, one launch (start us, length us, event | category | flops | bytes accessed | tf_op | source)
XLA Modules:
  0.0 163.1 jit_solution(6985295222898480150)
XLA Ops:
  0.0 2.7 %copy.19 = f32[4,16,8,768]{3,2,0,1:T(8,128)} copy(f32[4,16,8,768]{3,2,1,0:T(8,128)} %bitcast.24) | data formatting | bytes 3145728 | tf_op jit(solution)/shard_map/all_to_all | solution.py:10
  2.7 0.0 copy-start
  2.7 0.0 copy-start.1
  2.8 7.7 %all-to-all-start = ((f32[32,16,768]{2,0,1:T(8,128)}), f32[32,16,768]{2,0,1:T(8,128)S(1)}, u32[]{:S(2)}, u32[]{:S(2)}) async-start(f32[32,16,768]{2,0,1:T(8,128)} %bitcast.19), calls=%async_computation | async-start | bytes 3145728 | tf_op jit(solution)/shard_map/all_to_all | solution.py:10
  10.5 0.0 copy-done
  10.5 0.1 copy.11
  10.6 0.0 copy-done.1
  10.7 0.7 gather_fusion
  11.4 0.1 select_bitcast_fusion
  11.5 0.1 copy.12
  11.6 132.0 %all-gather = f32[256,2,256]{2,1,0:T(2,128)S(1)} all-gather(f32[1,2,256]{2,1,0:T(2,128)S(1)} %copy.12), channel_id=1, replica_groups=mesh['space'=16,'basis'=16] {'space','basis'}, dimensions={0}, use_global_device_ids=true | all-gather | bytes 526336 | tf_op jit(solution)/shard_map/all_gather | solution.py:9
  143.6 0.4 reshape.22
  143.9 0.2 copy.13
  144.1 0.0 all-to-all-done
  144.1 1.5 fusion
  145.6 16.6 %all_to_all.35 = f32[16,16,768]{2,1,0:T(8,128)S(1)} all-to-all(f32[16,16,768]{2,1,0:T(8,128)S(1)} %fusion), channel_id=1, replica_groups=mesh['space'=16,'basis'=16] {'basis'}, dimensions={0} | all-to-all | bytes 1572864 | tf_op jit(solution)/shard_map/all_to_all | solution.py:17
  162.2 0.9 copy.17
  (3 shorter events, 0.0 us)
Async XLA Ops:
  2.7 7.7 %copy-start = (f32[2,512]{1,0:T(2,128)S(1)}, f32[2,512]{1,0:T(2,128)}, u32[]{:S(2)}) copy-start(f32[2,512]{1,0:T(2,128)} %param.4) | copy-start | bytes 12292
  2.7 7.9 %copy-start.1 = (s32[256]{0:T(256)S(1)}, s32[256]{0:T(256)}, u32[]{:S(2)}) copy-start(s32[256]{0:T(256)} %param.5) | copy-start | bytes 3076
  2.8 141.4 %all-to-all-start = ((f32[32,16,768]{2,0,1:T(8,128)}), f32[32,16,768]{2,0,1:T(8,128)S(1)}, u32[]{:S(2)}, u32[]{:S(2)}) async-start(f32[32,16,768]{2,0,1:T(8,128)} %bitcast.19), calls=%async_computation | async-start | bytes 3145728 | tf_op jit(solution)/shard_map/all_to_all | solution.py:10

commit v2 on v1

v2 whole, which is shorter than its diff:
```python
import functools

import jax
import jax.numpy as jnp
from jax import lax
from jax.experimental import pallas as pl
from jax.experimental.pallas import tpu as pltpu
from jax.sharding import PartitionSpec as P

MESH = pl.DeviceIdType.MESH
NX, NY, NZ, NC = 4, 4, 8, 2
NB, NS = NX * NY, NZ * NC
CHUNKS = 3
PEERS = (
    (2, 2), (2, 1), (2, 3), (1, 2), (3, 2), (1, 1), (3, 3), (1, 3), (3, 1),
    (2, 0), (0, 2), (1, 0), (3, 0), (0, 1), (0, 3),
)
ZS = (1, 7, 2, 6, 3, 5, 4)


def kernel(basis, schur, kept, out, sel, k1, k2, kt, held, prod,
           b_send, b_recv, b_own, p_send, p_recv, p_own,
           s_send, s_recv, z_send, z_recv, f_send, f_recv):
    rows = basis.shape[0]
    own = out.shape[0]
    width = held.shape[3]
    block = CHUNKS * width
    space = lax.axis_index("space")
    me = lax.axis_index("basis")
    z, core = space // NC, lax.rem(space, NC)
    y, x = me // NX, lax.rem(me, NX)
    plane = [lax.rem(y + dy, NY) * NX + lax.rem(x + dx, NX) for dx, dy in PEERS]
    line = [lax.rem(z + d, NZ) for d in ZS]
    sibling = {"space": z * NC + 1 - core}

    barrier = pltpu.get_barrier_semaphore()
    for j in plane:
        pl.semaphore_signal(barrier, inc=1, device_id={"basis": j}, device_id_type=MESH)
    for zj in line:
        pl.semaphore_signal(barrier, inc=1, device_id={"space": zj * NC + core}, device_id_type=MESH)
    pl.semaphore_signal(barrier, inc=1, device_id=sibling, device_id_type=MESH)

    def columns(j, c):
        return pl.ds(pl.multiple_of(j * block + c * width, 128), width)

    for c in range(CHUNKS):
        pltpu.make_async_copy(basis.at[:, columns(me, c)], held.at[c, me], b_own.at[c]).start()

    index = lax.broadcasted_iota(jnp.int32, (schur.shape[1], kept.shape[1]), 0)
    one_hot = jnp.where(index == kept[...], 1.0, 0.0).astype(jnp.float32)
    sel[...] = jnp.dot(schur[...], one_hot, precision=lax.Precision.HIGHEST,
                       preferred_element_type=jnp.float32)

    pl.semaphore_wait(barrier, len(PEERS) + len(ZS) + 1)

    for j in plane:
        pltpu.make_async_remote_copy(
            src_ref=sel, dst_ref=k1.at[me], send_sem=s_send, recv_sem=s_recv,
            device_id={"basis": j}, device_id_type=MESH).start()

    def send_block(j, c):
        pltpu.make_async_remote_copy(
            src_ref=basis.at[:, columns(j, c)], dst_ref=held.at[c, me],
            send_sem=b_send.at[c], recv_sem=b_recv.at[c],
            device_id={"basis": j}, device_id_type=MESH).start()

    for j in plane:
        send_block(j, 0)

    k1[me] = sel[...]
    received = k1.at[pl.ds(0, NB - 1)]
    pltpu.make_async_copy(received, received, s_recv).wait()
    for j in range(NB):
        k2[z, core, 2 * j:2 * j + 2, :] = k1[j]
    mine = k2.at[z, core]
    for i, zj in enumerate(line):
        pltpu.make_async_remote_copy(
            src_ref=mine, dst_ref=mine, send_sem=z_send.at[i], recv_sem=z_recv.at[i],
            device_id={"space": zj * NC + core}, device_id_type=MESH).start()
    pltpu.make_async_remote_copy(
        src_ref=mine, dst_ref=mine, send_sem=f_send, recv_sem=f_recv,
        device_id=sibling, device_id_type=MESH).start()

    for c in range(1, CHUNKS):
        for j in plane:
            send_block(j, c)

    for i, d in enumerate(ZS):
        block_z = k2.at[lax.rem(z + NZ - d, NZ), core]
        pltpu.make_async_copy(block_z, block_z, z_recv.at[i]).wait()
        pltpu.make_async_remote_copy(
            src_ref=block_z, dst_ref=block_z, send_sem=f_send, recv_sem=f_recv,
            device_id=sibling, device_id_type=MESH).start()
    forwarded = k2.at[:, 0]
    pltpu.make_async_copy(forwarded, forwarded, f_recv).wait()
    kt[...] = k2[...].reshape(NS * rows, kept.shape[1]).T

    for c in range(CHUNKS):
        pltpu.make_async_copy(basis.at[:, columns(me, c)], held.at[c, me], b_own.at[c]).wait()
        others = held.at[c, pl.ds(0, NB - 1)]
        pltpu.make_async_copy(others, others, b_recv.at[c]).wait()
        result = jnp.dot(kt[...], held[c].reshape(NB * rows, width), precision=lax.Precision.HIGHEST,
                         preferred_element_type=jnp.float32)
        prod[c] = result.reshape(NB, own, width)
        for j in plane:
            pltpu.make_async_remote_copy(
                src_ref=prod.at[c, j], dst_ref=out.at[:, columns(me, c)],
                send_sem=p_send.at[c], recv_sem=p_recv.at[c],
                device_id={"basis": j}, device_id_type=MESH).start()
        pltpu.make_async_copy(prod.at[c, me], out.at[:, columns(me, c)], p_own.at[c]).start()

    pltpu.make_async_copy(received, received, s_send).wait()
    for i in range(len(ZS)):
        pltpu.make_async_copy(mine, mine, z_send.at[i]).wait()
    pltpu.make_async_copy(forwarded, forwarded, f_send).wait()
    for c in range(CHUNKS):
        others = held.at[c, pl.ds(0, NB - 1)]
        pltpu.make_async_copy(others, others, b_send.at[c]).wait()
        results = prod.at[c, pl.ds(0, NB - 1)]
        pltpu.make_async_copy(results, results, p_send.at[c]).wait()
        pltpu.make_async_copy(results, results, p_recv.at[c]).wait()
        pltpu.make_async_copy(prod.at[c, me], out.at[:, columns(me, c)], p_own.at[c]).wait()


def body(basis_block, schur, kept):
    rows, total = basis_block.shape
    picked = kept.shape[0]
    own = picked // NB
    width = total // NB // CHUNKS
    f32, vmem, dma = jnp.float32, pltpu.VMEM, pltpu.SemaphoreType.DMA
    return pl.pallas_call(
        kernel,
        out_shape=jax.ShapeDtypeStruct((own, total), f32),
        in_specs=[
            pl.BlockSpec(memory_space=pl.ANY),
            pl.BlockSpec(memory_space=vmem),
            pl.BlockSpec(memory_space=vmem),
        ],
        out_specs=pl.BlockSpec(memory_space=pl.ANY),
        scratch_shapes=[
            vmem((schur.shape[0], picked), f32),
            vmem((NB, schur.shape[0], picked), f32),
            vmem((NZ, NC, rows, picked), f32),
            vmem((picked, NB * rows), f32),
            vmem((CHUNKS, NB, rows, width), f32),
            vmem((CHUNKS, NB, own, width), f32),
            dma((CHUNKS,)), dma((CHUNKS,)), dma((CHUNKS,)),
            dma((CHUNKS,)), dma((CHUNKS,)), dma((CHUNKS,)),
            dma, dma, dma((len(ZS),)), dma((len(ZS),)), dma, dma,
        ],
        compiler_params=pltpu.CompilerParams(
            collective_id=0, has_side_effects=True, vmem_limit_bytes=40 << 20),
        cost_estimate=pl.CostEstimate(flops=2 * picked * NB * rows * width * CHUNKS, bytes_accessed=3 << 20, transcendentals=0),
    )(basis_block, schur, kept.reshape(1, picked))


def solution(mesh):
    in_specs = (P("basis", "space"), P(("space", "basis"), None), P())
    out_specs = P("basis", "space")
    return jax.shard_map(body, mesh=mesh, in_specs=in_specs, out_specs=out_specs, check_vma=False)
```

time: 164 us -> 41.3 us (0.25)
  blocking collectives: 149 us -> 0 us
  Pallas kernels: 0 us -> 37.5 us
  starting transfers between devices: 7.72 us -> 0 us
    all_gather x1 -> x0, blocking collectives: 132 us -> none  [body(): kept_full = lax.all_gather(selected, ('space', 'basis'), axis=0, tiled=True)]
    pallas_call x0 -> x1, Pallas kernels: none -> 37.5 us  [body(): pl.pallas_call(kernel, out_shape=jax.ShapeDtypeStruct((own, total), f32),...]
    all_to_all x1 -> x0, blocking collectives: 16.6 us -> none  [body(): lax.all_to_all(product, 'basis', split_axis=0, concat_axis=1, tiled=True)]
    all_to_all x1 -> x0, starting transfers between devices: 7.72 us -> none  [body(): lax.all_to_all(basis_block, 'basis', split_axis=1, concat_axis=0, tiled=T...]
    all_to_all x2 -> x0, local copies, waits for them, and re-layouts: 3.68 us -> none  [the longest x1 2.74 us: body(): lax.all_to_all(basis_block, 'basis', split_axis=1, concat_axis=0, tiled=T...]
    unnamed x7, local copies, waits for them, and re-layouts: 0.59 us -> 3.65 us
  transfers between devices with their start and end apart: 1 -> 0, of which waited for: 0 -> 0; matrix products, arithmetic and copies ran while one was open for 1% -> 0% of each run, Pallas kernels for 0% -> 0%
where the time goes in v2:
time: 41.3 us; the launch traced here: 41.2 us
  Pallas kernels  37.5 us (91%)
  local copies, waits for them, and re-layouts  3.65 us (9%)
    pallas_call x1, Pallas kernels, body(): pl.pallas_call(kernel, out_shape=jax.ShapeDtypeStruct((own, total), f32),...  37.5 us
    unnamed x7, local copies, waits for them, and re-layouts  3.65 us

profile of v2, /device:TPU:1, one launch (start us, length us, event | category | flops | bytes accessed | tf_op | source)
XLA Modules:
  0.0 41.2 jit_solution(5163503587155457393)
XLA Ops:
  0.0 0.0 copy-start
  0.0 1.4 %copy-done = f32[32,12288]{1,0:T(8,128)S(1)} copy-done((f32[32,12288]{1,0:T(8,128)S(1)}, f32[32,12288]{1,0:T(8,128)}, u32[]{:S(2)}) %copy-start) | copy-done | bytes 1572888
  1.4 0.0 copy-start.1
  1.4 0.7 %copy-done.1 = f32[2,512]{1,0:T(2,128)S(1)} copy-done((f32[2,512]{1,0:T(2,128)S(1)}, f32[2,512]{1,0:T(2,128)}, u32[]{:S(2)}) %copy-start.1) | copy-done | bytes 4120
  2.1 0.0 copy-start.2
  2.1 0.7 %copy-done.2 = s32[256]{0:T(256)S(1)} copy-done((s32[256]{0:T(256)S(1)}, s32[256]{0:T(256)}, u32[]{:S(2)}) %copy-start.2) | copy-done | bytes 1048
  2.8 37.5 %shard_map.37 = f32[16,12288]{1,0:T(8,128)S(1)} custom-call(f32[32,12288]{1,0:T(8,128)S(1)} %copy-done, f32[2,512]{1,0:T(2,128)S(1)} %copy-done.1, s32[1,256]{1,0:T(1,128)S(1)} %bitcast.1), custom_call_target="tpu_custom_call" | custom-call | flops 201326592 | bytes 3145728 | tf_op jit(solution)/shard_map/pallas_call | solution.py:131
  40.3 0.9 %copy.5 = f32[16,12288]{1,0:T(8,128)} copy(f32[16,12288]{1,0:T(8,128)S(1)} %shard_map.37) | data formatting | bytes 1572864
Async XLA Ops:
  0.0 1.4 %copy-start = (f32[32,12288]{1,0:T(8,128)S(1)}, f32[32,12288]{1,0:T(8,128)}, u32[]{:S(2)}) copy-start(f32[32,12288]{1,0:T(8,128)} %basis.1) | copy-start | bytes 4718596
  1.4 0.7 %copy-start.1 = (f32[2,512]{1,0:T(2,128)S(1)}, f32[2,512]{1,0:T(2,128)}, u32[]{:S(2)}) copy-start(f32[2,512]{1,0:T(2,128)} %schur.1) | copy-start | bytes 12292
  2.1 0.7 %copy-start.2 = (s32[256]{0:T(256)S(1)}, s32[256]{0:T(256)}, u32[]{:S(2)}) copy-start(s32[256]{0:T(256)} %param.5) | copy-start | bytes 3076

commit v3 on v2

--- a/solution.py
+++ b/solution.py
@@ -18,7 +18,7 @@
 ZS = (1, 7, 2, 6, 3, 5, 4)
 
 
-def kernel(basis, schur, kept, out, sel, k1, k2, kt, held, prod,
+def kernel(basis, schur_in, kept_in, out, schur, kept, in_sem, sel, k1, k2, kt, held, prod,
            b_send, b_recv, b_own, p_send, p_recv, p_own,
            s_send, s_recv, z_send, z_recv, f_send, f_recv):
     rows = basis.shape[0]
@@ -33,6 +33,12 @@
     line = [lax.rem(z + d, NZ) for d in ZS]
     sibling = {"space": z * NC + 1 - core}
 
+    loads = [
+        pltpu.make_async_copy(schur_in, schur, in_sem.at[0]),
+        pltpu.make_async_copy(kept_in, kept, in_sem.at[1]),
+    ]
+    for load in loads:
+        load.start()
     barrier = pltpu.get_barrier_semaphore()
     for j in plane:
         pl.semaphore_signal(barrier, inc=1, device_id={"basis": j}, device_id_type=MESH)
@@ -46,6 +52,8 @@
     for c in range(CHUNKS):
         pltpu.make_async_copy(basis.at[:, columns(me, c)], held.at[c, me], b_own.at[c]).start()
 
+    for load in loads:
+        load.wait()
     index = lax.broadcasted_iota(jnp.int32, (schur.shape[1], kept.shape[1]), 0)
     one_hot = jnp.where(index == kept[...], 1.0, 0.0).astype(jnp.float32)
     sel[...] = jnp.dot(schur[...], one_hot, precision=lax.Precision.HIGHEST,
@@ -130,14 +138,17 @@
     f32, vmem, dma = jnp.float32, pltpu.VMEM, pltpu.SemaphoreType.DMA
     return pl.pallas_call(
         kernel,
-        out_shape=jax.ShapeDtypeStruct((own, total), f32),
+        out_shape=vmem((own, total), f32),
         in_specs=[
-            pl.BlockSpec(memory_space=pl.ANY),
-            pl.BlockSpec(memory_space=vmem),
-            pl.BlockSpec(memory_space=vmem),
+            pl.BlockSpec(memory_space=pltpu.HBM),
+            pl.BlockSpec(memory_space=pltpu.HBM),
+            pl.BlockSpec(memory_space=pltpu.HBM),
         ],
         out_specs=pl.BlockSpec(memory_space=pl.ANY),
         scratch_shapes=[
+            vmem(schur.shape, f32),
+            vmem((1, picked), jnp.int32),
+            dma((2,)),
             vmem((schur.shape[0], picked), f32),
             vmem((NB, schur.shape[0], picked), f32),
             vmem((NZ, NC, rows, picked), f32),
@@ -151,7 +162,7 @@
         compiler_params=pltpu.CompilerParams(
             collective_id=0, has_side_effects=True, vmem_limit_bytes=40 << 20),
         cost_estimate=pl.CostEstimate(flops=2 * picked * NB * rows * width * CHUNKS, bytes_accessed=3 << 20, transcendentals=0),
-    )(basis_block, schur, kept.reshape(1, picked))
+    )(*(pltpu.with_memory_space_constraint(a, pltpu.HBM) for a in (basis_block, schur, kept.reshape(1, picked))))
 
 
 def solution(mesh):

time: 41.3 us -> 39.3 us (0.952)
  local copies, waits for them, and re-layouts: 3.65 us -> 0.88 us
  Pallas kernels: 37.5 us -> 38.3 us
    unnamed x7 -> x1, local copies, waits for them, and re-layouts: 3.65 us -> 0.88 us
    pallas_call x1, Pallas kernels: 37.5 us -> 38.3 us  [body(): pl.pallas_call(kernel, out_shape=vmem((own, total), f32), in_specs=[pl.Bl...]
where the time goes in v3:
time: 39.3 us; the launch traced here: 39.2 us
  Pallas kernels  38.3 us (97%)
  local copies, waits for them, and re-layouts  0.88 us (2%)
    pallas_call x1, Pallas kernels, body(): pl.pallas_call(kernel, out_shape=vmem((own, total), f32), in_specs=[pl.Bl...  38.3 us
    unnamed x1, local copies, waits for them, and re-layouts  0.88 us

profile of v3, /device:TPU:1, one launch (start us, length us, event | category | flops | bytes accessed | tf_op | source)
XLA Modules:
  0.0 39.2 jit_solution(10134943204586320546)
XLA Ops:
  0.0 38.3 %shard_map.37 = f32[16,12288]{1,0:T(8,128)S(1)} custom-call(f32[32,12288]{1,0:T(8,128)} %basis.1, f32[2,512]{1,0:T(2,128)} %schur_in.1, s32[1,256]{1,0:T(1,128)} %bitcast.1), custom_call_target="tpu_custom_call" | custom-call | flops 201326592 | bytes 3145728 | tf_op jit(solution)/shard_map/pallas_call | solution.py:139
  38.3 0.9 %copy.5 = f32[16,12288]{1,0:T(8,128)} copy(f32[16,12288]{1,0:T(8,128)S(1)} %shard_map.37) | data formatting | bytes 1572864

commit v4 on v1

v4 whole, which is shorter than its diff:
```python
import functools

import jax
import jax.numpy as jnp
from jax import lax
from jax.experimental import pallas as pl
from jax.experimental.pallas import tpu as pltpu
from jax.sharding import PartitionSpec as P

MESH = pl.DeviceIdType.MESH
NX, NY, NZ, NC = 4, 4, 8, 2
NB, NS = NX * NY, NZ * NC
SHARES = (2, 2, 2)
LANE = 128
PEERS = (
    (2, 2), (2, 1), (2, 3), (1, 2), (3, 2), (1, 1), (3, 3), (1, 3), (3, 1),
    (2, 0), (0, 2), (1, 0), (3, 0), (0, 1), (0, 3),
)
FIRST = 15


def kernel(basis, schur_in, kept_in, out, schur, kept, in_sem, sel, k1, k2, kt,
           b_send, b_recv, b_own, p_send, p_recv, p_own,
           s_send, s_recv, z_send, z_recv, f_send, f_recv, higher, *chunks):
    count = len(SHARES)
    held, prod = chunks[:count], chunks[count:]
    rows = basis.shape[0]
    own = out.shape[0]
    block = LANE * sum(SHARES)
    space = lax.axis_index("space")
    me = lax.axis_index("basis")
    z, core = space // NC, lax.rem(space, NC)
    y, x = me // NX, lax.rem(me, NX)
    plane = [lax.rem(y + dy, NY) * NX + lax.rem(x + dx, NX) for dx, dy in PEERS]
    def at(level):
        return {"space": level * NC + core}

    sibling = {"space": z * NC + 1 - core}

    def tell(sem, device):
        pl.semaphore_signal(sem, inc=1, device_id=device, device_id_type=MESH)

    def copy_to(device, src, dst, send, recv):
        pltpu.make_async_remote_copy(
            src_ref=src, dst_ref=dst, send_sem=send, recv_sem=recv,
            device_id=device, device_id_type=MESH).start()

    def wait_for(ref, sem):
        pltpu.make_async_copy(ref, ref, sem).wait()

    def columns(j, c):
        first = j * block + LANE * sum(SHARES[:c])
        return pl.ds(pl.multiple_of(first, LANE), LANE * SHARES[c])

    barrier = pltpu.get_barrier_semaphore()
    for j in plane:
        tell(barrier, {"basis": j})
    for level in range(1, NZ):
        @pl.when(level > z)
        def _():
            tell(barrier, at(level))

    @pl.when(core == 1)
    def _():
        tell(barrier, sibling)

    loads = [
        pltpu.make_async_copy(schur_in, schur, in_sem.at[0]),
        pltpu.make_async_copy(kept_in, kept, in_sem.at[1]),
    ]
    for load in loads:
        load.start()
    for c in range(count):
        pltpu.make_async_copy(basis.at[:, columns(me, c)], held[c].at[me], b_own.at[c]).start()
    for load in loads:
        load.wait()
    index = lax.broadcasted_iota(jnp.int32, (schur.shape[1], kept.shape[1]), 0)
    one_hot = jnp.where(index == kept[...], 1.0, 0.0).astype(jnp.float32)
    sel[...] = jnp.dot(schur[...], one_hot, precision=lax.Precision.HIGHEST,
                       preferred_element_type=jnp.float32)

    pl.semaphore_wait(barrier, NB - 1 + z + 1 - core)
    for j in plane:
        copy_to({"basis": j}, sel, k1.at[me], s_send, s_recv)

    def send_blocks(first, last):
        for c, j in [(c, j) for c in range(count) for j in plane][first:last]:
            copy_to({"basis": j}, basis.at[:, columns(j, c)], held[c].at[me], b_send.at[c], b_recv.at[c])

    send_blocks(0, FIRST)

    for level in range(NZ - 1):
        @pl.when(level < z)
        def _():
            tell(higher, at(level))

    @pl.when(core == 0)
    def _():
        tell(higher, sibling)

    k1[me] = sel[...]
    received = k1.at[pl.ds(0, NB - 1)]
    wait_for(received, s_recv)
    for j in range(NB):
        k2[z, core, 2 * j:2 * j + 2, :] = k1[j]
    mine = k2.at[z, core]

    def send_level(level):
        d = lax.rem(level + NZ - z, NZ) - 1
        copy_to(at(level), mine, mine, z_send.at[d], z_recv.at[d])

    for level in range(NZ - 1):
        @pl.when(level < z)
        def _():
            send_level(level)

    send_blocks(FIRST, None)

    expected = NZ - 1 - z + core

    @pl.when(expected > 0)
    def _():
        pl.semaphore_wait(higher, expected)

    for level in range(1, NZ):
        @pl.when(level > z)
        def _():
            send_level(level)
    copy_to(sibling, mine, mine, f_send, f_recv)

    for level in range(NZ):
        @pl.when(level != z)
        def _():
            passed = k2.at[level, core]
            wait_for(passed, z_recv.at[lax.rem(z + NZ - level, NZ) - 1])
            copy_to(sibling, passed, passed, f_send, f_recv)
    forwarded = k2.at[:, 0]
    wait_for(forwarded, f_recv)
    kt[...] = k2[...].reshape(NS * rows, kept.shape[1]).T

    for c in range(count):
        pltpu.make_async_copy(basis.at[:, columns(me, c)], held[c].at[me], b_own.at[c]).wait()
        wait_for(held[c].at[pl.ds(0, NB - 1)], b_recv.at[c])
        result = jnp.dot(kt[...], held[c][...].reshape(NB * rows, -1), precision=lax.Precision.HIGHEST,
                         preferred_element_type=jnp.float32)
        prod[c][...] = result.reshape(NB, own, -1)
        for j in plane:
            copy_to({"basis": j}, prod[c].at[j], out.at[:, columns(me, c)], p_send.at[c], p_recv.at[c])
        pltpu.make_async_copy(prod[c].at[me], out.at[:, columns(me, c)], p_own.at[c]).start()

    wait_for(received, s_send)
    for d in range(NZ - 1):
        wait_for(mine, z_send.at[d])
    wait_for(forwarded, f_send)
    for c in range(count):
        wait_for(held[c].at[pl.ds(0, NB - 1)], b_send.at[c])
        results = prod[c].at[pl.ds(0, NB - 1)]
        wait_for(results, p_send.at[c])
        wait_for(results, p_recv.at[c])
        pltpu.make_async_copy(prod[c].at[me], out.at[:, columns(me, c)], p_own.at[c]).wait()


def body(basis_block, schur, kept):
    rows, total = basis_block.shape
    picked = kept.shape[0]
    own = picked // NB
    f32, vmem, dma = jnp.float32, pltpu.VMEM, pltpu.SemaphoreType.DMA
    regular = pltpu.SemaphoreType.REGULAR
    count = len(SHARES)
    operands = (basis_block, schur, kept.reshape(1, picked))
    return pl.pallas_call(
        kernel,
        out_shape=vmem((own, total), f32),
        in_specs=[pl.BlockSpec(memory_space=pltpu.HBM)] * 3,
        out_specs=pl.BlockSpec(memory_space=pl.ANY),
        scratch_shapes=[
            vmem(schur.shape, f32),
            vmem((1, picked), jnp.int32),
            dma((2,)),
            vmem((schur.shape[0], picked), f32),
            vmem((NB, schur.shape[0], picked), f32),
            vmem((NZ, NC, rows, picked), f32),
            vmem((picked, NB * rows), f32),
            dma((count,)), dma((count,)), dma((count,)),
            dma((count,)), dma((count,)), dma((count,)),
            dma, dma, dma((NZ - 1,)), dma((NZ - 1,)), dma, dma,
            regular,
            *(vmem((NB, rows, LANE * s), f32) for s in SHARES),
            *(vmem((NB, own, LANE * s), f32) for s in SHARES),
        ],
        compiler_params=pltpu.CompilerParams(
            collective_id=0, has_side_effects=True, vmem_limit_bytes=40 << 20),
        cost_estimate=pl.CostEstimate(flops=2 * picked * rows * total, bytes_accessed=3 << 20, transcendentals=0),
    )(*(pltpu.with_memory_space_constraint(a, pltpu.HBM) for a in operands))


def solution(mesh):
    in_specs = (P("basis", "space"), P(("space", "basis"), None), P())
    out_specs = P("basis", "space")
    return jax.shard_map(body, mesh=mesh, in_specs=in_specs, out_specs=out_specs, check_vma=False)
```

time: 164 us -> 36.7 us (0.22)
  blocking collectives: 149 us -> 0 us
  Pallas kernels: 0 us -> 35.7 us
  starting transfers between devices: 7.72 us -> 0 us
  local copies, waits for them, and re-layouts: 5.19 us -> 0.88 us
    all_gather x1 -> x0, blocking collectives: 132 us -> none  [body(): kept_full = lax.all_gather(selected, ('space', 'basis'), axis=0, tiled=True)]
    pallas_call x0 -> x1, Pallas kernels: none -> 35.7 us  [body(): pl.pallas_call(kernel, out_shape=vmem((own, total), f32), in_specs=[pl.Bl...]
    all_to_all x1 -> x0, blocking collectives: 16.6 us -> none  [body(): lax.all_to_all(product, 'basis', split_axis=0, concat_axis=1, tiled=True)]
    all_to_all x1 -> x0, starting transfers between devices: 7.72 us -> none  [body(): lax.all_to_all(basis_block, 'basis', split_axis=1, concat_axis=0, tiled=T...]
    all_to_all x2 -> x0, local copies, waits for them, and re-layouts: 3.68 us -> none  [the longest x1 2.74 us: body(): lax.all_to_all(basis_block, 'basis', split_axis=1, concat_axis=0, tiled=T...]
  transfers between devices with their start and end apart: 1 -> 0, of which waited for: 0 -> 0; matrix products, arithmetic and copies ran while one was open for 1% -> 0% of each run, Pallas kernels for 0% -> 0%
where the time goes in v4:
time: 36.7 us; the launch traced here: 36.5 us
  Pallas kernels  35.7 us (97%)
  local copies, waits for them, and re-layouts  0.88 us (2%)
    pallas_call x1, Pallas kernels, body(): pl.pallas_call(kernel, out_shape=vmem((own, total), f32), in_specs=[pl.Bl...  35.7 us
    unnamed x1, local copies, waits for them, and re-layouts  0.88 us

profile of v4, /device:TPU:1, one launch (start us, length us, event | category | flops | bytes accessed | tf_op | source)
XLA Modules:
  0.0 36.5 jit_solution(14830570597216591844)
XLA Ops:
  0.0 35.7 %shard_map.37 = f32[16,12288]{1,0:T(8,128)S(1)} custom-call(f32[32,12288]{1,0:T(8,128)} %basis.1, f32[2,512]{1,0:T(2,128)} %schur_in.1, s32[1,256]{1,0:T(1,128)} %bitcast.1), custom_call_target="tpu_custom_call" | custom-call | flops 201326592 | bytes 3145728 | tf_op jit(solution)/shard_map/pallas_call | solution.py:171
  35.7 0.9 %copy.5 = f32[16,12288]{1,0:T(8,128)} copy(f32[16,12288]{1,0:T(8,128)S(1)} %shard_map.37) | data formatting | bytes 1572864

commit v5 on v4

--- a/solution.py
+++ b/solution.py
@@ -10,13 +10,13 @@
 MESH = pl.DeviceIdType.MESH
 NX, NY, NZ, NC = 4, 4, 8, 2
 NB, NS = NX * NY, NZ * NC
-SHARES = (2, 2, 2)
+SHARES = (1, 2, 1, 2)
 LANE = 128
 PEERS = (
     (2, 2), (2, 1), (2, 3), (1, 2), (3, 2), (1, 1), (3, 3), (1, 3), (3, 1),
     (2, 0), (0, 2), (1, 0), (3, 0), (0, 1), (0, 3),
 )
-FIRST = 15
+FIRST = 30
 
 
 def kernel(basis, schur_in, kept_in, out, schur, kept, in_sem, sel, k1, k2, kt,

time: 36.7 us -> 35.6 us (0.970)
  Pallas kernels: 35.7 us -> 34.6 us
    pallas_call x1, Pallas kernels: 35.7 us -> 34.6 us  [body(): pl.pallas_call(kernel, out_shape=vmem((own, total), f32), in_specs=[pl.Bl...]
where the time goes in v5:
time: 35.6 us; the launch traced here: 35.4 us
  Pallas kernels  34.6 us (97%)
  local copies, waits for them, and re-layouts  0.88 us (2%)
    pallas_call x1, Pallas kernels, body(): pl.pallas_call(kernel, out_shape=vmem((own, total), f32), in_specs=[pl.Bl...  34.6 us
    unnamed x1, local copies, waits for them, and re-layouts  0.88 us

profile of v5, /device:TPU:1, one launch (start us, length us, event | category | flops | bytes accessed | tf_op | source)
XLA Modules:
  0.0 35.4 jit_solution(17538329461445699254)
XLA Ops:
  0.0 34.6 %shard_map.37 = f32[16,12288]{1,0:T(8,128)S(1)} custom-call(f32[32,12288]{1,0:T(8,128)} %basis.1, f32[2,512]{1,0:T(2,128)} %schur_in.1, s32[1,256]{1,0:T(1,128)} %bitcast.1), custom_call_target="tpu_custom_call" | custom-call | flops 201326592 | bytes 3145728 | tf_op jit(solution)/shard_map/pallas_call | solution.py:171
  34.6 0.9 %copy.5 = f32[16,12288]{1,0:T(8,128)} copy(f32[16,12288]{1,0:T(8,128)S(1)} %shard_map.37) | data formatting | bytes 1572864

commit v6 on v5

--- a/solution.py
+++ b/solution.py
@@ -16,7 +16,9 @@
     (2, 2), (2, 1), (2, 3), (1, 2), (3, 2), (1, 1), (3, 3), (1, 3), (3, 1),
     (2, 0), (0, 2), (1, 0), (3, 0), (0, 1), (0, 3),
 )
-FIRST = 30
+FIRST = 22
+SECOND = 30
+AHEAD = 1
 
 
 def kernel(basis, schur_in, kept_in, out, schur, kept, in_sem, sel, k1, k2, kt,
@@ -114,7 +116,7 @@
         def _():
             send_level(level)
 
-    send_blocks(FIRST, None)
+    send_blocks(FIRST, SECOND)
 
     expected = NZ - 1 - z + core
 
@@ -126,32 +128,61 @@
         @pl.when(level > z)
         def _():
             send_level(level)
-    copy_to(sibling, mine, mine, f_send, f_recv)
-
-    for level in range(NZ):
-        @pl.when(level != z)
-        def _():
-            passed = k2.at[level, core]
-            wait_for(passed, z_recv.at[lax.rem(z + NZ - level, NZ) - 1])
-            copy_to(sibling, passed, passed, f_send, f_recv)
-    forwarded = k2.at[:, 0]
-    wait_for(forwarded, f_recv)
-    kt[...] = k2[...].reshape(NS * rows, kept.shape[1]).T
-
-    for c in range(count):
+    copy_to(sibling, mine, mine, f_send.at[0], f_recv.at[0])
+    send_blocks(SECOND, None)
+
+
+    levels = NZ // 2
+    blocks = NB // 2
+    quota = k2.at[pl.ds(0, levels), 0]
+
+    def take_rows(part):
+        half = lax.rem(z // levels + part, 2)
+        for i in range(levels):
+            level = half * levels + i
+
+            @pl.when(level != z)
+            def _():
+                passed = k2.at[level, core]
+                wait_for(passed, z_recv.at[lax.rem(z + NZ - level, NZ) - 1])
+                copy_to(sibling, passed, passed, f_send.at[part], f_recv.at[part])
+
+        wait_for(quota, f_recv.at[part])
+        kt[part] = k2[pl.ds(half * levels, levels)].reshape(blocks * rows, kept.shape[1]).T
+
+    def multiply(c, part):
+        half = lax.rem(z // levels + part, 2)
+        vectors = held[c][pl.ds(half * blocks, blocks)].reshape(blocks * rows, -1)
+        result = jnp.dot(kt[part], vectors, precision=lax.Precision.HIGHEST, preferred_element_type=jnp.float32)
+        return result.reshape(NB, own, -1)
+
+    def take_chunk(c):
         pltpu.make_async_copy(basis.at[:, columns(me, c)], held[c].at[me], b_own.at[c]).wait()
         wait_for(held[c].at[pl.ds(0, NB - 1)], b_recv.at[c])
-        result = jnp.dot(kt[...], held[c][...].reshape(NB * rows, -1), precision=lax.Precision.HIGHEST,
-                         preferred_element_type=jnp.float32)
-        prod[c][...] = result.reshape(NB, own, -1)
+
+    def send_results(c):
         for j in plane:
             copy_to({"basis": j}, prod[c].at[j], out.at[:, columns(me, c)], p_send.at[c], p_recv.at[c])
         pltpu.make_async_copy(prod[c].at[me], out.at[:, columns(me, c)], p_own.at[c]).start()
 
+    take_rows(0)
+    for c in range(AHEAD):
+        take_chunk(c)
+        prod[c][...] = multiply(c, 0)
+    take_rows(1)
+    for c in range(AHEAD):
+        prod[c][...] += multiply(c, 1)
+        send_results(c)
+    for c in range(AHEAD, count):
+        take_chunk(c)
+        prod[c][...] = multiply(c, 0) + multiply(c, 1)
+        send_results(c)
+
     wait_for(received, s_send)
     for d in range(NZ - 1):
         wait_for(mine, z_send.at[d])
-    wait_for(forwarded, f_send)
+    for part in range(2):
+        wait_for(quota, f_send.at[part])
     for c in range(count):
         wait_for(held[c].at[pl.ds(0, NB - 1)], b_send.at[c])
         results = prod[c].at[pl.ds(0, NB - 1)]
@@ -180,10 +211,10 @@
             vmem((schur.shape[0], picked), f32),
             vmem((NB, schur.shape[0], picked), f32),
             vmem((NZ, NC, rows, picked), f32),
-            vmem((picked, NB * rows), f32),
+            vmem((2, picked, NB * rows // 2), f32),
             dma((count,)), dma((count,)), dma((count,)),
             dma((count,)), dma((count,)), dma((count,)),
-            dma, dma, dma((NZ - 1,)), dma((NZ - 1,)), dma, dma,
+            dma, dma, dma((NZ - 1,)), dma((NZ - 1,)), dma((2,)), dma((2,)),
             regular,
             *(vmem((NB, rows, LANE * s), f32) for s in SHARES),
             *(vmem((NB, own, LANE * s), f32) for s in SHARES),

time: 35.6 us -> 35 us (0.983)
  Pallas kernels: 34.6 us -> 34 us
    pallas_call x1, Pallas kernels: 34.6 us -> 34 us  [body(): pl.pallas_call(kernel, out_shape=vmem((own, total), f32), in_specs=[pl.Bl...]
where the time goes in v6:
time: 35 us; the launch traced here: 34.9 us
  Pallas kernels  34 us (97%)
  local copies, waits for them, and re-layouts  0.88 us (3%)
    pallas_call x1, Pallas kernels, body(): pl.pallas_call(kernel, out_shape=vmem((own, total), f32), in_specs=[pl.Bl...  34 us
    unnamed x1, local copies, waits for them, and re-layouts  0.88 us

profile of v6, /device:TPU:1, one launch (start us, length us, event | category | flops | bytes accessed | tf_op | source)
XLA Modules:
  0.0 34.9 jit_solution(12129190524649313246)
XLA Ops:
  0.0 34.0 %shard_map.37 = f32[16,12288]{1,0:T(8,128)S(1)} custom-call(f32[32,12288]{1,0:T(8,128)} %basis.1, f32[2,512]{1,0:T(2,128)} %schur_in.1, s32[1,256]{1,0:T(1,128)} %bitcast.1), custom_call_target="tpu_custom_call" | custom-call | flops 201326592 | bytes 3145728 | tf_op jit(solution)/shard_map/pallas_call | solution.py:202
  34.0 0.9 %copy.5 = f32[16,12288]{1,0:T(8,128)} copy(f32[16,12288]{1,0:T(8,128)S(1)} %shard_map.37) | data formatting | bytes 1572864

commit v7 on v6

--- a/solution.py
+++ b/solution.py
@@ -16,8 +16,8 @@
     (2, 2), (2, 1), (2, 3), (1, 2), (3, 2), (1, 1), (3, 3), (1, 3), (3, 1),
     (2, 0), (0, 2), (1, 0), (3, 0), (0, 1), (0, 3),
 )
-FIRST = 22
-SECOND = 30
+FIRST = 24
+SECOND = 45
 AHEAD = 1
 
 
@@ -82,6 +82,16 @@
                        preferred_element_type=jnp.float32)
 
     pl.semaphore_wait(barrier, NB - 1 + z + 1 - core)
+
+    for level in range(NZ - 1):
+        @pl.when(level < z)
+        def _():
+            tell(higher, at(level))
+
+    @pl.when(core == 0)
+    def _():
+        tell(higher, sibling)
+
     for j in plane:
         copy_to({"basis": j}, sel, k1.at[me], s_send, s_recv)
 
@@ -90,15 +100,6 @@
             copy_to({"basis": j}, basis.at[:, columns(j, c)], held[c].at[me], b_send.at[c], b_recv.at[c])
 
     send_blocks(0, FIRST)
-
-    for level in range(NZ - 1):
-        @pl.when(level < z)
-        def _():
-            tell(higher, at(level))
-
-    @pl.when(core == 0)
-    def _():
-        tell(higher, sibling)
 
     k1[me] = sel[...]
     received = k1.at[pl.ds(0, NB - 1)]

time: 35 us -> 35.1 us (level)
  no operation moved by 1% of the time
where the time goes in v7:
time: 35.1 us; the launch traced here: 34.9 us
  Pallas kernels  34 us (97%)
  local copies, waits for them, and re-layouts  0.88 us (3%)
    pallas_call x1, Pallas kernels, body(): pl.pallas_call(kernel, out_shape=vmem((own, total), f32), in_specs=[pl.Bl...  34 us
    unnamed x1, local copies, waits for them, and re-layouts  0.88 us

profile of v7, /device:TPU:1, one launch (start us, length us, event | category | flops | bytes accessed | tf_op | source)
XLA Modules:
  0.0 34.9 jit_solution(5155723243738894126)
XLA Ops:
  0.0 34.0 %shard_map.37 = f32[16,12288]{1,0:T(8,128)S(1)} custom-call(f32[32,12288]{1,0:T(8,128)} %basis.1, f32[2,512]{1,0:T(2,128)} %schur_in.1, s32[1,256]{1,0:T(1,128)} %bitcast.1), custom_call_target="tpu_custom_call" | custom-call | flops 201326592 | bytes 3145728 | tf_op jit(solution)/shard_map/pallas_call | solution.py:203
  34.1 0.9 %copy.5 = f32[16,12288]{1,0:T(8,128)} copy(f32[16,12288]{1,0:T(8,128)S(1)} %shard_map.37) | data formatting | bytes 1572864

commit v8 on v6

--- a/solution.py
+++ b/solution.py
@@ -33,7 +33,8 @@
     me = lax.axis_index("basis")
     z, core = space // NC, lax.rem(space, NC)
     y, x = me // NX, lax.rem(me, NX)
-    plane = [lax.rem(y + dy, NY) * NX + lax.rem(x + dx, NX) for dx, dy in PEERS]
+    turn = 1 - 2 * core
+    plane = [lax.rem(y + turn * dy + NY, NY) * NX + lax.rem(x + turn * dx + NX, NX) for dx, dy in PEERS]
     def at(level):
         return {"space": level * NC + core}
 

time: 35 us -> 35 us (level)
  no operation moved by 1% of the time
where the time goes in v8:
time: 35 us; the launch traced here: 34.9 us
  Pallas kernels  34 us (97%)
  local copies, waits for them, and re-layouts  0.88 us (3%)
    pallas_call x1, Pallas kernels, body(): pl.pallas_call(kernel, out_shape=vmem((own, total), f32), in_specs=[pl.Bl...  34 us
    unnamed x1, local copies, waits for them, and re-layouts  0.88 us

profile of v8, /device:TPU:1, one launch (start us, length us, event | category | flops | bytes accessed | tf_op | source)
XLA Modules:
  0.0 34.9 jit_solution(2337012870016821897)
XLA Ops:
  0.0 34.0 %shard_map.37 = f32[16,12288]{1,0:T(8,128)S(1)} custom-call(f32[32,12288]{1,0:T(8,128)} %basis.1, f32[2,512]{1,0:T(2,128)} %schur_in.1, s32[1,256]{1,0:T(1,128)} %bitcast.1), custom_call_target="tpu_custom_call" | custom-call | flops 201326592 | bytes 3145728 | tf_op jit(solution)/shard_map/pallas_call | solution.py:203
  34.0 0.9 %copy.5 = f32[16,12288]{1,0:T(8,128)} copy(f32[16,12288]{1,0:T(8,128)S(1)} %shard_map.37) | data formatting | bytes 1572864
